TPU v7x, 256 devices: a whole 4x4x8 slice. The times are simulated.
256 devices in a mesh: row: 32 (over z, y), col: 8 (over x, core).
Axes of the slice: x: 4, y: 4, z: 8, core: 2. Of those that a mesh axis runs over, the one named last changes fastest.
Arguments:
- tokens: bfloat16 [4096, 5120], P('row', 'col'), may hold values from -6 to 6
- target: bfloat16 [4096, 5120], P('row', 'col'), may hold values from -6 to 6
- w_gate: bfloat16 [5120, 13824], P('col', 'row'), may hold values from -0.078125 to 0.078125
- w_up: bfloat16 [5120, 13824], P('col', 'row'), may hold values from -0.078125 to 0.078125
- w_down: bfloat16 [13824, 5120], P('row', 'col'), may hold values from -0.0546875 to 0.0546875
- factor_u: bfloat16 [5120, 256], P('col'), may hold values from -0.078125 to 0.078125
- factor_v: bfloat16 [256, 13824], P(None, 'row'), may hold values from -3 to 3
Outputs:
- mixed: bfloat16 [4096, 5120], P('row', 'col')
- fitness: float32 [64], replicated
- update: float32 [5120, 13824], P('col', 'row')
All inputs are finite; a program needn't handle non-finite values.
Results may differ from a plain program's by a relative error of at most 0.0049.
Values may be sent and summed in bfloat16 or wider, within the bound.
No kernel may reach another device: no remote copies, remote signals or barrier semaphores. Data moves between devices by JAX's collectives and lax.ppermute only.
A program may use at most 128 MiB of HBM per device.

v0:
```python
import math
import jax
import jax.numpy as jnp
from jax import lax
from jax.sharding import PartitionSpec as P

D = 5120
RANK = 4
SEQ = 64
sigma_scale = 0.5


def apply_factors(low_three, v_three):
    return jnp.einsum("psr,prf->psf", low_three, v_three, precision=lax.Precision.HIGHEST)


def body(tokens, target, w_gate, w_up, w_down, factor_u, factor_v):
    dev_rows, dev_feat = tokens.shape
    members = factor_u.shape[1] // RANK
    units = w_up.shape[1]
    every = lax.all_gather(tokens, "row", axis=0, tiled=True)
    total_rows = every.shape[0]
    gate_part = jnp.dot(every, w_gate, preferred_element_type=jnp.float32)
    up_part = jnp.dot(every, w_up, preferred_element_type=jnp.float32)
    grouped = every.reshape(members, SEQ, dev_feat)
    u_three = factor_u.reshape(dev_feat, members, RANK)
    v_three = factor_v.reshape(members, RANK, units).astype(jnp.float32)
    low_part = jnp.einsum("psd,dpr->psr", grouped, u_three, preferred_element_type=jnp.float32)
    up_part = up_part + sigma_scale * apply_factors(low_part, v_three).reshape(total_rows, units)
    gate, up = (
        lax.psum_scatter(gate_part, "col", scatter_dimension=0, tiled=True),
        lax.psum_scatter(up_part, "col", scatter_dimension=0, tiled=True),
    )
    hidden = (jax.nn.silu(gate) * up).astype(jnp.bfloat16)
    hidden_all = lax.all_gather(hidden, "col", axis=0, tiled=True)
    out = lax.psum_scatter(
        jnp.dot(hidden_all, w_down, preferred_element_type=jnp.float32),
        "row",
        scatter_dimension=0,
        tiled=True,
    )
    mixed = out.astype(jnp.bfloat16)
    local_members = dev_rows // SEQ
    prod = (out * target.astype(jnp.float32)).reshape(local_members, SEQ * dev_feat)
    score = jnp.sum(prod, axis=1) / math.sqrt(SEQ * D)
    placed = lax.dynamic_update_slice(
        jnp.zeros((members,), jnp.float32), score, (lax.axis_index("row") * local_members,)
    )
    fitness = lax.psum(placed, ("row", "col"))
    weights = jnp.repeat(fitness, RANK)
    update = jnp.dot(
        factor_u.astype(jnp.float32) * weights[None, :],
        factor_v.astype(jnp.float32),
        precision=lax.Precision.HIGHEST,
        preferred_element_type=jnp.float32,
    ) * math.sqrt(D / members)
    return (mixed, fitness, update)


def solution(mesh):
    return jax.shard_map(
        body,
        mesh=mesh,
        in_specs=(
            P("row", "col"),
            P("row", "col"),
            P("col", "row"),
            P("col", "row"),
            P("row", "col"),
            P("col", None),
            P(None, "row"),
        ),
        out_specs=(P("row", "col"), P(), P("col", "row")),
        check_vma=False,
    )
```

profile of v0, /device:TPU:1, one launch (start us, length us, event | category | flops | bytes accessed | tf_op | source)
XLA Modules:
  0.0 587.6 jit_solution(11700659747309950121)
XLA Ops:
  7.2 0.0 copy-start
  7.2 0.0 all-gather.3.cloned.1.call-start
  7.2 0.7 all-gather.3.cloned.1.call-update
  7.9 0.0 reduce-scatter.6.cloned.1.call-start
  8.0 1.2 copy.12
  9.1 0.1 reshape.22
  9.2 1.1 copy.13
  10.3 0.1 reshape.23
  10.4 86.9 %all-gather.3.cloned.1.call-done = bf16[4096,640]{1,0:T(8,128)(2,1)} async-done(((bf16[128,640]{1,0:T(8,128)(2,1)}), bf16[4096,640]{1,0:T(8,128)(2,1)}) %all-gather.3.cloned.1.call-update) | async-done | bytes 5242896 | tf_op jit(solution)/shard_map/all_gather | solution.py:21
  97.3 4.2 fusion.4
  101.5 5.8 broadcast_multiply_fusion
  107.3 0.0 copy-start.3
  107.3 8.6 %copy.14 = f32[4096,432]{0,1:T(8,128)} copy(f32[4096,432]{1,0:T(8,128)} %bitcast.15) | data formatting | bytes 14155776 | tf_op jit(solution)/shard_map/mul | solution.py:29
  115.9 0.0 copy-done.3
  115.9 9.4 %convolution_add_fusion = f32[4096,432]{0,1:T(8,128)} fusion(f32[4096,432]{0,1:T(8,128)} %copy.14, bf16[4096,640]{1,0:T(8,128)(2,1)} %all-gather.3.cloned.1.call-done, bf16[640,432]{0,1:T(8,128)(2,1)S(1)} %copy-done.3), kind=kOutput, calls=%fused_computation | convolution fusion | flops 2266693632 | bytes 19951616 | tf_op jit(solution)/shard_map/dot_general | solution.py:24
  125.3 0.0 copy-start.6
  125.3 0.0 reduce-scatter.6.cloned.1.call-update
  125.4 0.0 reduce-scatter.4.cloned.1.call-start
  125.4 1.0 copy-done.6
  126.4 8.3 %fusion.3 = f32[4096,432]{0,1:T(8,128)} fusion(bf16[4096,640]{1,0:T(8,128)(2,1)} %all-gather.3.cloned.1.call-done, bf16[640,432]{0,1:T(8,128)(2,1)S(1)} %copy-done.6), kind=kOutput, calls=%fused_computation.9 | convolution fusion | flops 2264924160 | bytes 12873728 | tf_op jit(solution)/shard_map/dot_general | solution.py:23
  134.7 0.0 reduce-scatter.4.cloned.1.call-update
  134.7 0.0 all-gather.5.cloned.1.call-start
  134.8 38.4 %reduce-scatter.6.cloned.1.call-done = f32[512,432]{0,1:T(8,128)} async-done(((f32[4096,432]{0,1:T(8,128)}), f32[512,432]{0,1:T(8,128)}) %reduce-scatter.6.cloned.1.call-update) | async-done | bytes 884752 | tf_op jit(solution)/shard_map/reduce_scatter | solution.py:32
  173.2 51.0 %reduce-scatter.4.cloned.1.call-done = f32[512,432]{0,1:T(8,128)} async-done(((f32[4096,432]{0,1:T(8,128)}), f32[512,432]{0,1:T(8,128)}) %reduce-scatter.4.cloned.1.call-update) | async-done | bytes 884752 | tf_op jit(solution)/shard_map/reduce_scatter | solution.py:31
  224.2 2.5 multiply_convert_fusion
  226.6 0.0 all-gather.5.cloned.1.call-update
  226.6 0.0 reduce-scatter.8.cloned.1.call-start
  226.7 32.6 %all-gather.5.cloned.1.call-done = bf16[4096,432]{0,1:T(8,128)(2,1)} async-done(((bf16[512,432]{0,1:T(8,128)(2,1)}), bf16[4096,432]{0,1:T(8,128)(2,1)}) %all-gather.5.cloned.1.call-update) | async-done | bytes 3538960 | tf_op jit(solution)/shard_map/all_gather | solution.py:35
  259.3 0.0 copy-done
  259.3 9.5 %fusion.5 = f32[4096,640]{1,0:T(8,128)} fusion(bf16[4096,432]{0,1:T(8,128)(2,1)} %all-gather.5.cloned.1.call-done, bf16[432,640]{1,0:T(8,128)(2,1)S(1)} %copy-done), kind=kOutput, calls=%fused_computation.11 | convolution fusion | flops 2264924160 | bytes 14577664 | tf_op jit(solution)/shard_map/dot_general | solution.py:37
  268.8 0.0 copy-start.4
  268.8 0.0 copy-start.1
  268.8 0.0 copy-start.2
  268.8 0.0 reduce-scatter.8.cloned.1.call-update
  268.8 229.8 %reduce-scatter.8.cloned.1.call-done = f32[128,640]{1,0:T(8,128)} async-done(((f32[4096,640]{1,0:T(8,128)}), f32[128,640]{1,0:T(8,128)}) %reduce-scatter.8.cloned.1.call-update) | async-done | bytes 327696 | tf_op jit(solution)/shard_map/reduce_scatter | solution.py:36
  498.6 0.0 copy-done.4
  498.6 1.8 multiply_reduce_fusion
  500.4 0.1 reduce_sum.14
  500.5 0.1 reduce_sum.18
  500.6 0.1 multiply_dynamic-update-slice_fusion
  500.7 78.4 %psum.7 = f32[64]{0:T(128)S(1)} all-reduce(f32[64]{0:T(128)S(1)} %multiply_dynamic-update-slice_fusion), channel_id=1, replica_groups=mesh['row'=32,'col'=8] {'row','col'}, use_global_device_ids=true, to_apply=%region_5.6 | all-reduce | flops 64 | bytes 512 | tf_op jit(solution)/shard_map/psum | solution.py:49
  579.1 0.0 copy-start.5
  579.1 0.1 broadcast_in_dim.7
  579.2 0.1 mul.45
  579.3 0.0 copy-done.1
  579.3 0.0 copy-done.2
  579.3 1.8 convolution_multiply_fusion
  581.1 0.0 copy-done.5
  (1 shorter events, 0.0 us)
Async XLA Ops:
  7.2 252.2 %copy-start = (bf16[432,640]{1,0:T(8,128)(2,1)S(1)}, bf16[432,640]{1,0:T(8,128)(2,1)}, u32[]{:S(2)}) copy-start(bf16[432,640]{1,0:T(8,128)(2,1)} %param.11) | copy-start | bytes 1658884
  7.2 90.1 %all-gather.3.cloned.1.call-start = ((), (), s32[]{:S(2)}) async-start(), calls=%async_computation.3 | async-start | bytes 5406720 | tf_op jit(solution)/shard_map/all_gather | solution.py:21
  7.9 165.3 %reduce-scatter.6.cloned.1.call-start = ((), (), s32[]{:S(2)}) async-start(), calls=%async_computation.5 | async-start | bytes 7962624 | tf_op jit(solution)/shard_map/reduce_scatter | solution.py:32
  107.3 8.7 %copy-start.3 = (bf16[640,432]{0,1:T(8,128)(2,1)S(1)}, bf16[640,432]{0,1:T(8,128)(2,1)}, u32[]{:S(2)}) copy-start(bf16[640,432]{0,1:T(8,128)(2,1)} %param.10) | copy-start | bytes 1658884
  125.3 1.1 copy-start.6
  125.4 98.8 %reduce-scatter.4.cloned.1.call-start = ((), (), s32[]{:S(2)}) async-start(), calls=%async_computation.4 | async-start | bytes 7962624 | tf_op jit(solution)/shard_map/reduce_scatter | solution.py:31
  134.7 124.6 %all-gather.5.cloned.1.call-start = ((), (), s32[]{:S(2)}) async-start(), calls=%async_computation.6 | async-start | bytes 3981312 | tf_op jit(solution)/shard_map/all_gather | solution.py:35
  226.6 272.0 %reduce-scatter.8.cloned.1.call-start = ((), (), s32[]{:S(2)}) async-start(), calls=%async_computation.7 | async-start | bytes 10813440 | tf_op jit(solution)/shard_map/reduce_scatter | solution.py:36
  268.8 229.8 %copy-start.4 = (bf16[128,640]{1,0:T(8,128)(2,1)S(1)}, bf16[128,640]{1,0:T(8,128)(2,1)}, u32[]{:S(2)}) copy-start(bf16[128,640]{1,0:T(8,128)(2,1)} %param.8) | copy-start | bytes 491524
  268.8 310.5 %copy-start.1 = (bf16[640,256]{1,0:T(8,128)(2,1)S(1)}, bf16[640,256]{1,0:T(8,128)(2,1)}, u32[]{:S(2)}) copy-start(bf16[640,256]{1,0:T(8,128)(2,1)} %param.12) | copy-start | bytes 983044
  268.8 310.5 %copy-start.2 = (bf16[256,432]{0,1:T(8,128)(2,1)S(1)}, bf16[256,432]{0,1:T(8,128)(2,1)}, u32[]{:S(2)}) copy-start(bf16[256,432]{0,1:T(8,128)(2,1)} %param.13) | copy-start | bytes 663556
  579.1 2.0 copy-start.5
Sparse Core Ops, SparseCore 0:
  10.6 86.6 all-gather.2
  125.5 47.6 reduce-scatter.5
  175.8 48.3 reduce-scatter.3
  226.8 32.5 all-gather.4
  268.9 229.6 reduce-scatter.7
where the time goes:
time: 588 us
  waiting for transfers between devices  439 us (75%)
  blocking collectives  78.4 us (13%)
  matrix products  39 us (7%)
  between operations  13.8 us (2%)
  local copies, waits for them, and re-layouts  12.3 us (2%)
    reduce_scatter x1, waiting for transfers between devices, body(): lax.psum_scatter(jnp.dot(hidden_all, w_down, preferred_element_type=jnp.f...  230 us
    all_gather x1, waiting for transfers between devices, body(): every = lax.all_gather(tokens, 'row', axis=0, tiled=True)  86.9 us
    psum x1, blocking collectives, body(): fitness = lax.psum(placed, ('row', 'col'))  78.4 us
    reduce_scatter x1, waiting for transfers between devices, body(): lax.psum_scatter(gate_part, 'col', scatter_dimension=0, tiled=True)  51 us
    reduce_scatter x1, waiting for transfers between devices, body(): lax.psum_scatter(up_part, 'col', scatter_dimension=0, tiled=True)  38.4 us
    all_gather x1, waiting for transfers between devices, body(): hidden_all = lax.all_gather(hidden, 'col', axis=0, tiled=True)  32.6 us
  transfers between devices with their start and end apart: 5, of which 5 were waited for; matrix products, arithmetic and copies ran while one was open for 2% of the time, Pallas kernels for 0%

commit v1 on v0

--- a/solution.py
+++ b/solution.py
@@ -18,7 +18,9 @@
     dev_rows, dev_feat = tokens.shape
     members = factor_u.shape[1] // RANK
     units = w_up.shape[1]
-    every = lax.all_gather(tokens, "row", axis=0, tiled=True)
+    every = jnp.concatenate(
+        lax.all_to_all(jnp.stack([tokens] * lax.axis_size("row")), "row", 0, 0), axis=0
+    )
     total_rows = every.shape[0]
     gate_part = jnp.dot(every, w_gate, preferred_element_type=jnp.float32)
     up_part = jnp.dot(every, w_up, preferred_element_type=jnp.float32)

time: 588 us -> 634 us (1.078)
  waiting for transfers between devices: 439 us -> 470 us
  starting transfers between devices: 0.2 us -> 12.4 us
    all_to_all x0 -> x1, waiting for transfers between devices: none -> 114 us  [body(): lax.all_to_all(jnp.stack([tokens] * lax.axis_size('row')), 'row', 0, 0)]
    all_gather x1 -> x0, waiting for transfers between devices: 86.9 us -> none  [body(): every = lax.all_gather(tokens, 'row', axis=0, tiled=True)]
    all_to_all x0 -> x1, starting transfers between devices: none -> 12.3 us  [body(): lax.all_to_all(jnp.stack([tokens] * lax.axis_size('row')), 'row', 0, 0)]
  transfers between devices with their start and end apart: 5 -> 5, of which waited for: 5 -> 5; matrix products, arithmetic and copies ran while one was open for 2% -> 1% of each run, Pallas kernels for 0% -> 0%
where the time goes in v1:
time: 634 us; the launch traced here: 633 us
  waiting for transfers between devices  470 us (74%)
  blocking collectives  78.5 us (12%)
  matrix products  38.9 us (6%)
  local copies, waits for them, and re-layouts  14.4 us (2%)
  between operations  13.8 us (2%)
  starting transfers between devices  12.4 us (2%)
    reduce_scatter x1, waiting for transfers between devices, body(): lax.psum_scatter(jnp.dot(hidden_all, w_down, preferred_element_type=jnp.f...  230 us
    all_to_all x1, waiting for transfers between devices, body(): lax.all_to_all(jnp.stack([tokens] * lax.axis_size('row')), 'row', 0, 0)  114 us
    psum x1, blocking collectives, body(): fitness = lax.psum(placed, ('row', 'col'))  78.5 us
    reduce_scatter x1, waiting for transfers between devices, body(): lax.psum_scatter(gate_part, 'col', scatter_dimension=0, tiled=True)  50.9 us
    reduce_scatter x1, waiting for transfers between devices, body(): lax.psum_scatter(up_part, 'col', scatter_dimension=0, tiled=True)  43 us
    all_gather x1, waiting for transfers between devices, body(): hidden_all = lax.all_gather(hidden, 'col', axis=0, tiled=True)  32.6 us
  transfers between devices with their start and end apart: 5, of which 5 were waited for; matrix products, arithmetic and copies ran while one was open for 1% of the time, Pallas kernels for 0%

profile of v1, /device:TPU:1, one launch (start us, length us, event | category | flops | bytes accessed | tf_op | source)
XLA Modules:
  0.0 633.0 jit_solution(10957261019408826684)
XLA Ops:
  7.2 0.0 copy-start
  7.2 4.0 stack.2
  11.2 0.0 copy-start.1
  11.2 0.0 copy-start.2
  11.2 12.3 %all-to-all-start = ((bf16[32,128,640]{2,1,0:T(8,128)(2,1)}), bf16[32,128,640]{2,1,0:T(8,128)(2,1)}, u32[]{:S(2)}, u32[]{:S(2)}) async-start(bf16[32,128,640]{2,1,0:T(8,128)(2,1)} %stack.2), calls=%async_computation | async-start | bytes 10485760 | tf_op jit(solution)/shard_map/all_to_all | solution.py:22
  23.5 0.0 reduce-scatter.6.cloned.1.call-start
  23.5 0.0 copy-done.1
  23.5 0.2 copy.12
  23.7 0.1 reshape.24
  23.8 0.0 copy-done.2
  23.8 0.1 copy.13
  24.0 0.1 reshape.25
  24.0 113.9 %all-to-all-done = bf16[32,128,640]{2,1,0:T(8,128)(2,1)} async-done(((bf16[32,128,640]{2,1,0:T(8,128)(2,1)}), bf16[32,128,640]{2,1,0:T(8,128)(2,1)}, u32[]{:S(2)}, u32[]{:S(2)}) %all-to-all-start) | async-done | bytes 5242912 | tf_op jit(solution)/shard_map/all_to_all | solution.py:22
  138.0 4.2 fusion.4
  142.2 5.8 broadcast_multiply_fusion
  148.0 0.0 copy-start.3
  148.0 8.7 %copy.14 = f32[4096,432]{0,1:T(8,128)} copy(f32[4096,432]{1,0:T(8,128)} %bitcast.16) | data formatting | bytes 14155776 | tf_op jit(solution)/shard_map/mul | solution.py:31
  156.6 0.0 copy-done.3
  156.7 9.4 %convolution_add_fusion = f32[4096,432]{0,1:T(8,128)} fusion(f32[4096,432]{0,1:T(8,128)} %copy.14, bf16[4096,640]{1,0:T(8,128)(2,1)} %bitcast, bf16[640,432]{0,1:T(8,128)(2,1)S(1)} %copy-done.3), kind=kOutput, calls=%fused_computation | convolution fusion | flops 2266693632 | bytes 19951616 | tf_op jit(solution)/shard_map/dot_general | solution.py:26
  166.1 0.0 copy-start.6
  166.1 0.0 reduce-scatter.6.cloned.1.call-update
  166.1 0.0 reduce-scatter.4.cloned.1.call-start
  166.2 1.0 copy-done.6
  167.1 8.3 %fusion.3 = f32[4096,432]{0,1:T(8,128)} fusion(bf16[4096,640]{1,0:T(8,128)(2,1)} %bitcast, bf16[640,432]{0,1:T(8,128)(2,1)S(1)} %copy-done.6), kind=kOutput, calls=%fused_computation.9 | convolution fusion | flops 2264924160 | bytes 12873728 | tf_op jit(solution)/shard_map/dot_general | solution.py:25
  175.4 0.0 reduce-scatter.4.cloned.1.call-update
  175.5 0.0 all-gather.2.cloned.1.call-start
  175.5 43.0 %reduce-scatter.6.cloned.1.call-done = f32[512,432]{0,1:T(8,128)} async-done(((f32[4096,432]{0,1:T(8,128)}), f32[512,432]{0,1:T(8,128)}) %reduce-scatter.6.cloned.1.call-update) | async-done | bytes 884752 | tf_op jit(solution)/shard_map/reduce_scatter | solution.py:34
  218.6 50.9 %reduce-scatter.4.cloned.1.call-done = f32[512,432]{0,1:T(8,128)} async-done(((f32[4096,432]{0,1:T(8,128)}), f32[512,432]{0,1:T(8,128)}) %reduce-scatter.4.cloned.1.call-update) | async-done | bytes 884752 | tf_op jit(solution)/shard_map/reduce_scatter | solution.py:33
  269.5 2.5 multiply_convert_fusion
  272.0 0.0 all-gather.2.cloned.1.call-update
  272.0 0.0 reduce-scatter.8.cloned.1.call-start
  272.0 32.6 %all-gather.2.cloned.1.call-done = bf16[4096,432]{0,1:T(8,128)(2,1)} async-done(((bf16[512,432]{0,1:T(8,128)(2,1)}), bf16[4096,432]{0,1:T(8,128)(2,1)}) %all-gather.2.cloned.1.call-update) | async-done | bytes 3538960 | tf_op jit(solution)/shard_map/all_gather | solution.py:37
  304.7 0.0 copy-done
  304.7 9.4 %fusion.5 = f32[4096,640]{1,0:T(8,128)} fusion(bf16[4096,432]{0,1:T(8,128)(2,1)} %all-gather.2.cloned.1.call-done, bf16[432,640]{1,0:T(8,128)(2,1)S(1)} %copy-done), kind=kOutput, calls=%fused_computation.11 | convolution fusion | flops 2264924160 | bytes 14577664 | tf_op jit(solution)/shard_map/dot_general | solution.py:39
  314.1 0.0 copy-start.4
  314.1 0.0 reduce-scatter.8.cloned.1.call-update
  314.1 229.8 %reduce-scatter.8.cloned.1.call-done = f32[128,640]{1,0:T(8,128)} async-done(((f32[4096,640]{1,0:T(8,128)}), f32[128,640]{1,0:T(8,128)}) %reduce-scatter.8.cloned.1.call-update) | async-done | bytes 327696 | tf_op jit(solution)/shard_map/reduce_scatter | solution.py:38
  543.9 0.0 copy-done.4
  544.0 1.8 multiply_reduce_fusion
  545.7 0.1 reduce_sum.14
  545.8 0.1 reduce_sum.18
  545.9 0.1 multiply_dynamic-update-slice_fusion
  546.0 78.5 %psum.7 = f32[64]{0:T(128)S(1)} all-reduce(f32[64]{0:T(128)S(1)} %multiply_dynamic-update-slice_fusion), channel_id=1, replica_groups=mesh['row'=32,'col'=8] {'row','col'}, use_global_device_ids=true, to_apply=%region_5.6 | all-reduce | flops 64 | bytes 512 | tf_op jit(solution)/shard_map/psum | solution.py:51
  624.5 0.0 copy-start.5
  624.5 0.1 broadcast_in_dim.7
  624.6 0.1 mul.45
  624.7 1.8 convolution_multiply_fusion
  626.5 0.0 copy-done.5
  (1 shorter events, 0.0 us)
Async XLA Ops:
  7.2 297.5 %copy-start = (bf16[432,640]{1,0:T(8,128)(2,1)S(1)}, bf16[432,640]{1,0:T(8,128)(2,1)}, u32[]{:S(2)}) copy-start(bf16[432,640]{1,0:T(8,128)(2,1)} %param.11) | copy-start | bytes 1658884
  11.2 12.3 %copy-start.1 = (bf16[640,256]{1,0:T(8,128)(2,1)S(1)}, bf16[640,256]{1,0:T(8,128)(2,1)}, u32[]{:S(2)}) copy-start(bf16[640,256]{1,0:T(8,128)(2,1)} %param.12) | copy-start | bytes 983044
  11.2 12.6 %copy-start.2 = (bf16[256,432]{0,1:T(8,128)(2,1)S(1)}, bf16[256,432]{0,1:T(8,128)(2,1)}, u32[]{:S(2)}) copy-start(bf16[256,432]{0,1:T(8,128)(2,1)} %param.13) | copy-start | bytes 663556
  11.2 126.8 %all-to-all-start = ((bf16[32,128,640]{2,1,0:T(8,128)(2,1)}), bf16[32,128,640]{2,1,0:T(8,128)(2,1)}, u32[]{:S(2)}, u32[]{:S(2)}) async-start(bf16[32,128,640]{2,1,0:T(8,128)(2,1)} %stack.2), calls=%async_computation | async-start | bytes 10485760 | tf_op jit(solution)/shard_map/all_to_all | solution.py:22
  23.5 195.1 %reduce-scatter.6.cloned.1.call-start = ((), (), s32[]{:S(2)}) async-start(), calls=%async_computation.5 | async-start | bytes 7962624 | tf_op jit(solution)/shard_map/reduce_scatter | solution.py:34
  148.0 8.7 %copy-start.3 = (bf16[640,432]{0,1:T(8,128)(2,1)S(1)}, bf16[640,432]{0,1:T(8,128)(2,1)}, u32[]{:S(2)}) copy-start(bf16[640,432]{0,1:T(8,128)(2,1)} %param.10) | copy-start | bytes 1658884
  166.1 1.1 copy-start.6
  166.1 103.4 %reduce-scatter.4.cloned.1.call-start = ((), (), s32[]{:S(2)}) async-start(), calls=%async_computation.4 | async-start | bytes 7962624 | tf_op jit(solution)/shard_map/reduce_scatter | solution.py:33
  175.5 129.2 %all-gather.2.cloned.1.call-start = ((), (), s32[]{:S(2)}) async-start(), calls=%async_computation.6 | async-start | bytes 3981312 | tf_op jit(solution)/shard_map/all_gather | solution.py:37
  272.0 272.0 %reduce-scatter.8.cloned.1.call-start = ((), (), s32[]{:S(2)}) async-start(), calls=%async_computation.7 | async-start | bytes 10813440 | tf_op jit(solution)/shard_map/reduce_scatter | solution.py:38
  314.1 229.8 %copy-start.4 = (bf16[128,640]{1,0:T(8,128)(2,1)S(1)}, bf16[128,640]{1,0:T(8,128)(2,1)}, u32[]{:S(2)}) copy-start(bf16[128,640]{1,0:T(8,128)(2,1)} %param.8) | copy-start | bytes 491524
  624.5 2.0 copy-start.5
Sparse Core Ops, SparseCore 0:
  166.2 52.2 reduce-scatter.5
  221.1 48.3 reduce-scatter.3
  272.1 32.5 all-gather.1
  314.3 229.6 reduce-scatter.7
